TPU v7x, 32 devices: a whole 2x2x4 slice. The times are simulated.
32 devices in a mesh: groups: 2 (over x), strip: 16 (over z, y, core).
Axes of the slice: x: 2, y: 2, z: 4, core: 2. Of those that a mesh axis runs over, the one named last changes fastest.
Arguments:
- x_tiles: bfloat16 [128, 2, 32, 32, 128], P(('groups', 'strip')), parts along dimension 0, may hold values from -6 to 6
- grad_out: bfloat16 [128, 2, 32, 32, 128], P(('groups', 'strip')), parts along dimension 0, may hold values from -6 to 6
- tile_pos: int32 [128], P(('groups', 'strip')), parts along dimension 0, may hold values from -1 to 3, as said below
- w_spatial: bfloat16 [9, 128, 128], replicated, may hold values from -0.1875 to 0.1875
- conv_bias: float32 [128], replicated, may hold values from -3 to 3
- w_temporal: bfloat16 [3, 128, 128], replicated, may hold values from -0.3125 to 0.3125
Outputs:
- grad_in: bfloat16 [128, 2, 32, 32, 128], P(('groups', 'strip')), parts along dimension 0
- d_spatial: float32 [18, 128, 128], P('groups'), parts along dimension 0
- d_temporal: float32 [6, 128, 128], P('groups'), parts along dimension 0
- d_bias: float32 [256], P('groups'), parts along dimension 0
There are 2 independent parts, one for each index of `groups`. A program takes and returns all parts, laid end to end along the dimension named above; an argument that names none is the same for every part. Nothing has to cross between parts.
Inputs may be any that keep to these rules, and one draw needn't show every extreme that they name: `tile_pos`: entries d * 4 to d * 4 + 3 belong to strip d: the distinct columns of its active tiles come first, then -1. Every strip has at least one active tile and some strips are wholly active. The first entries of neighbouring strips differ by at most one.
All inputs are finite; a program needn't handle non-finite values.
Results may differ from a plain program's by a relative error of at most 0.0049.
Values may be sent and summed in bfloat16 or wider, within the bound.
A program may use at most 64 MiB of HBM per device.

v0:
```python
import jax
import jax.numpy as jnp
from jax import lax
from jax.sharding import PartitionSpec as P

FORWARD = [(a, b) for a in range(3) for b in range(3)]
BACKWARD = [(2 - a, 2 - b) for a in range(3) for b in range(3)]


def padded_2(array, sides, width):
    for axis, dim in sides:
        size, length = (lax.axis_size(axis), array.shape[dim])
        up = [(i, (i + 1) % size) for i in range(size - 1)]
        down = [(j, i) for i, j in up]
        last = lax.slice_in_dim(array, length - width, length, axis=dim)
        first = lax.slice_in_dim(array, 0, width, axis=dim)
        before = lax.ppermute(last, axis, up)
        after = lax.ppermute(first, axis, down)
        array = jnp.concatenate([before, array, after], axis=dim)
    return array


def silu_pair(values):
    sigmoid = jax.nn.sigmoid(values)
    return (values * sigmoid, sigmoid * (1.0 + values * (1.0 - sigmoid)))


def spatial_columns(padded, offsets):
    height = padded.shape[1] - 2
    pieces = [padded[:, a : a + height, b : b + height, :] for a, b in offsets]
    return jnp.concatenate(pieces, axis=-1).reshape(-1, 9 * padded.shape[-1])


def backward_terms(padded, grad_tile, spatial_stack, conv_bias, temporal_back):
    frames = grad_tile.shape[0]
    channels = grad_tile.shape[-1]
    columns = spatial_columns(padded, FORWARD)
    pre_act = jnp.dot(columns, spatial_stack, preferred_element_type=jnp.float32) + conv_bias
    activation, act_slope = silu_pair(pre_act)
    hidden = activation.astype(jnp.bfloat16).reshape(frames, -1, channels)
    grad_rows = grad_tile.reshape(frames, -1, channels)
    frame_pad = ((1, 1), (0, 0), (0, 0))
    grad_pad = jnp.pad(grad_rows, frame_pad)
    hidden_pad = jnp.pad(hidden, frame_pad)
    grad_taps = jnp.concatenate(
        [grad_pad[2 - k : 2 - k + frames] for k in range(3)], axis=-1
    ).reshape(-1, 3 * channels)
    hidden_taps = jnp.concatenate([hidden_pad[k : k + frames] for k in range(3)], axis=-1).reshape(
        -1, 3 * channels
    )
    grad_hidden = jnp.dot(grad_taps, temporal_back, preferred_element_type=jnp.float32)
    grad_pre = (grad_hidden * act_slope).astype(jnp.bfloat16)
    temporal_term = jnp.dot(
        hidden_taps.T, grad_rows.reshape(-1, channels), preferred_element_type=jnp.float32
    )
    spatial_term = jnp.dot(columns.T, grad_pre, preferred_element_type=jnp.float32)
    bias_term = jnp.sum(lax.optimization_barrier(grad_pre).astype(jnp.float32), axis=0)
    return (grad_pre.reshape(grad_tile.shape), (spatial_term, temporal_term, bias_term))


def dense_row(tile_data, tile_pos, row_number):
    edge_cells = jnp.transpose(tile_data[:, :, row_number], (1, 0, 2, 3))
    target = jnp.where(tile_pos >= 0, tile_pos, tile_pos.shape[0])
    placed = (
        jnp.zeros(edge_cells.shape, edge_cells.dtype).at[:, target].set(edge_cells, mode="drop")
    )
    return placed.reshape(edge_cells.shape[0], -1, edge_cells.shape[-1])


def dense_column(tile_data, tile_pos, col_number):
    edge_cells = tile_data[:, :, :, col_number]
    target = jnp.where(tile_pos >= 0, tile_pos + 1, tile_pos.shape[0] + 2)
    shape_out = (tile_pos.shape[0] + 2,) + edge_cells.shape[1:]
    return jnp.zeros(shape_out, edge_cells.dtype).at[target].set(edge_cells, mode="drop")


def surround_tiles(tile_data, tile_pos, above_row, below_row):
    height = tile_data.shape[2]
    column = jnp.maximum(tile_pos, 0)
    side_pad = ((0, 0), (1, 1), (0, 0))
    above_pad = jnp.pad(above_row, side_pad)
    below_pad = jnp.pad(below_row, side_pad)

    def cut_rows(source):
        return jax.vmap(lambda offset: lax.dynamic_slice_in_dim(source, offset, height + 2, 1))(
            column * height
        )

    top_rows = cut_rows(above_pad)
    bottom_rows = cut_rows(below_pad)
    left_cols = dense_column(tile_data, tile_pos, height - 1)[column]
    right_cols = dense_column(tile_data, tile_pos, 0)[column + 2]
    middle = jnp.concatenate(
        [left_cols[:, :, :, None], tile_data, right_cols[:, :, :, None]], axis=3
    )
    return jnp.concatenate([top_rows[:, :, None], middle, bottom_rows[:, :, None]], axis=2)


def first_pass(padded_all, grad_all, begin, finish, pre_grads, partial_value, weights):
    spatial_stack, conv_bias, temporal_back = weights

    def advance(which_slot, carried):
        buffer_now, sums_now = carried
        grad_pre, tile_terms = backward_terms(
            padded_all[which_slot], grad_all[which_slot], spatial_stack, conv_bias, temporal_back
        )
        buffer_now = lax.dynamic_update_index_in_dim(buffer_now, grad_pre, which_slot, 0)
        return (buffer_now, tuple((s + t for s, t in zip(sums_now, tile_terms))))

    return lax.fori_loop(begin, finish, advance, (pre_grads, partial_value))


def per_device(x_tiles, grad_out, tile_pos, w_spatial, conv_bias, w_temporal):
    slot_count = x_tiles.shape[0]
    frames = x_tiles.shape[1]
    height = x_tiles.shape[2]
    channels = x_tiles.shape[4]
    weights = (
        w_spatial.reshape(9 * channels, channels),
        conv_bias,
        jnp.transpose(w_temporal, (0, 2, 1)).reshape(3 * channels, channels),
    )
    spatial_back = jnp.transpose(w_spatial, (0, 2, 1)).reshape(9 * channels, channels)
    active_count = jnp.sum((tile_pos >= 0).astype(jnp.int32))
    last_row = height - 1
    edge_rows = jnp.stack(
        [dense_row(x_tiles, tile_pos, 0), dense_row(x_tiles, tile_pos, last_row)], axis=1
    )
    reached = padded_2(edge_rows, (("strip", 1),), 1)
    above_row, below_row = (reached[:, 0], reached[:, 3])
    padded_x = surround_tiles(x_tiles, tile_pos, above_row, below_row)
    partial_value = (
        jnp.zeros((9 * channels, channels), jnp.float32),
        jnp.zeros((3 * channels, channels), jnp.float32),
        jnp.zeros((channels,), jnp.float32),
    )
    pre_grads = jnp.zeros_like(x_tiles)
    pre_grads, partial_value = first_pass(
        padded_x, grad_out, 0, active_count, pre_grads, partial_value, weights
    )
    totals = lax.psum(partial_value, "strip")
    grad_edges = jnp.stack(
        [dense_row(pre_grads, tile_pos, 0), dense_row(pre_grads, tile_pos, last_row)], axis=1
    )
    reached_grad = padded_2(grad_edges, (("strip", 1),), 1)
    above_grad, below_grad = (reached_grad[:, 0], reached_grad[:, 3])
    padded_grad = surround_tiles(pre_grads, tile_pos, above_grad, below_grad)

    def second(which_slot, result):
        columns = spatial_columns(padded_grad[which_slot], BACKWARD)
        tile_grad = jnp.dot(columns, spatial_back, preferred_element_type=jnp.float32).astype(
            jnp.bfloat16
        )
        return lax.dynamic_update_index_in_dim(
            result, tile_grad.reshape(frames, height, height, channels), which_slot, 0
        )

    grad_in = lax.fori_loop(0, active_count, second, jnp.zeros_like(x_tiles))
    scale_factor = float(lax.axis_size("strip") * slot_count * frames * height * height) ** (-0.5)
    d_spatial = (totals[0] * scale_factor).reshape(9, channels, channels)
    d_temporal = (totals[1] * scale_factor).reshape(3, channels, channels)
    d_bias = totals[2] * scale_factor
    return (grad_in, d_spatial, d_temporal, d_bias)


def solution(mesh):
    in_specs = (
        P(("groups", "strip"), None, None, None, None),
        P(("groups", "strip"), None, None, None, None),
        P(("groups", "strip")),
        P(),
        P(),
        P(),
    )
    out_specs = (
        P(("groups", "strip"), None, None, None, None),
        P("groups", None, None),
        P("groups", None, None),
        P("groups"),
    )
    return jax.shard_map(
        per_device, mesh=mesh, in_specs=in_specs, out_specs=out_specs, check_vma=False
    )
```

profile of v0, /device:TPU:0, one launch (start us, length us, event | category | flops | bytes accessed | tf_op | source)
XLA Modules:
  0.0 210.4 jit_solution(1110457826979658469)
XLA Ops:
  7.2 1.5 broadcast_maximum_fusion
  10.4 2.4 %collective-permute-start = (bf16[2,1,128,128]{3,0,2,1:T(2,128)(2,1)S(1)}, bf16[2,1,128,128]{3,0,2,1:T(2,128)(2,1)S(1)}, u32[]{:S(2)}, u32[]{:S(2)}) collective-permute-start(bf16[2,1,128,128]{3,0,2,1:T(2,128)(2,1)S(1)} %copy.17), channel_id=1, source_target_pairs={{0,1},{1,2},{2,3},{3,4},{4,5},{5,6},{6,7},{7,8},{8,9},{9,10},{10,1... | collective-permute-start | bytes 196616 | tf_op jit(solution)/shard_map/ppermute | solution.py:17
  13.5 1.3 collective-permute-start.1
  14.8 1.5 fusion.20
  19.1 1.6 copy.16
  20.7 1.2 copy.33
  23.6 2.6 %pad_maximum_fusion = bf16[4,2,34,34,128]{4,3,2,1,0:T(8,128)(2,1)} fusion(bf16[4,2,1,34,128]{4,3,2,1,0:T(8,128)(2,1)S(1)} %copy.24, bf16[4,2,32,1,128]{4,3,2,1,0:T(2,128)(2,1)S(1)} %copy.21, bf16[4,2,32,32,128]{4,3,2,1,0:T(8,128)(2,1)S(1)} %copy-done.1, bf16[4,2,32,1,128]{4,3,2,1,0:T(2,128)(2,1)S(1)} %copy.20, bf16[4,2,1,34,128]{4,3,2,1,0:T(8,128)(2,1)S(1)} %copy.23), kind=kLoop, calls=%fused_computation.65 | loop fusion | flops 11837440 | bytes 4734976 | tf_op jit(solution)/shard_map/concatenate | solution.py:96
  26.7 10.3 %while.28 = (s32[]{:T(128)}, bf16[4,2,32,32,128]{4,3,2,1,0:T(8,128)(2,1)S(1)}, f32[1152,128]{1,0:T(8,128)S(1)}, f32[384,128]{1,0:T(8,128)S(1)}, f32[128]{0:T(128...) while((s32[]{:T(128)}, ...), condition=%wide.region_7.8_spmd, body=%wide.region_5.7_spmd.sunk | while | flops 1624702976 | bytes 35529448 | solution.py:110
  27.3 1.2 dynamic-slice_bitcast_fusion.4
  30.4 1.5 multiply_convert_fusion.2
  31.9 1.1 constant_dynamic-slice_fusion.2
  34.5 1.5 convolution_add_fusion.3
  39.7 15.5 %collective-permute-start.2 = (bf16[2,1,128,128]{3,0,2,1:T(2,128)(2,1)}, bf16[2,1,128,128]{3,0,2,1:T(2,128)(2,1)}, u32[]{:S(2)}, u32[]{:S(2)}) collective-permute-start(bf16[2,1,128,128]{3,0,2,1:T(2,128)(2,1)} %copy.25), channel_id=1, source_target_pairs={{0,1},{1,2},{2,3},{3,4},{4,5},{5,6},{6,7},{7,8},{8,9},{9,10},{10,1... | collective-permute-start | bytes 196616 | tf_op jit(solution)/shard_map/ppermute | solution.py:17
  56.6 1.3 collective-permute-start.3
  57.9 50.5 %psum.23 = f32[128]{0:T(128)S(1)} all-reduce(f32[128]{0:T(128)} %copy-done.8), channel_id=1, replica_groups=mesh['groups'=2,'strip'=16] {'strip'}, use_global_device_ids=true, to_apply=%region_16.17 | all-reduce | flops 128 | bytes 1024 | tf_op jit(solution)/shard_map/psum | solution.py:141
  111.8 0.9 pad.28
  113.4 0.9 pad.29
  115.0 2.6 %pad_maximum_fusion.1 = bf16[4,2,34,34,128]{4,3,2,1,0:T(8,128)(2,1)} fusion(bf16[4,2,1,34,128]{4,3,2,1,0:T(8,128)(2,1)S(1)} %copy.32, bf16[4,2,32,1,128]{4,3,2,1,0:T(2,128)(2,1)S(1)} %copy.29, bf16[4,2,32,32,128]{4,3,2,1,0:T(8,128)(2,1)S(1)} %get-tuple-element.175, bf16[4,2,32,1,128]{4,3,2,1,0:T(2,128)(2,1)S(1)} %copy.28, ...), kind=kLoop, calls=%fused_computation.66 | loop fusion | flops 11837440 | bytes 4734976 | tf_op jit(solution)/shard_map/concatenate | solution.py:96
  118.0 5.7 %while.29 = (s32[]{:T(128)}, bf16[4,2,32,32,128]{4,3,2,1,0:T(8,128)(2,1)S(1)}, s32[]{:T(128)}, bf16[4,2,34,34,128]{4,3,2,1,0:T(8,128)(2,1)}, bf16[1152,128]{1,0:...) while((s32[]{:T(128)}, bf16[4,2,32,32,128]{4,3,2,1,0:T(8,128)(2,1)S(1)}, s32[]{:T(128)}, ...), condition=%wide.region_13.14_spmd, body=%wide.region_12.13_spmd.sunk | while | flops 604241920 | bytes 17207424 | solution.py:158
  118.7 1.2 dynamic-slice_bitcast_fusion.5
  121.6 1.4 convolution_convert_fusion.2
  123.8 76.2 %all-reduce.9.cloned.1.call-done = (f32[1152,128]{1,0:T(8,128)}, f32[384,128]{1,0:T(8,128)}) async-done(((f32[1152,128]{1,0:T(8,128)}, f32[384,128]{1,0:T(8,128)}), (f32[1152,128]{1,0:T(8,128)}, f32[384,128]{1,0:T(8,128)})) %all-reduce.9.cloned.1.call-update) | async-done | bytes 786448 | tf_op jit(solution)/shard_map/psum | solution.py:141
  200.0 1.9 broadcast_multiply_fusion
  201.9 1.6 broadcast_multiply_fusion.1
  (100 shorter events, 21.8 us)
Async XLA Ops:
  7.2 16.4 %copy-start.1 = (bf16[4,2,32,32,128]{4,3,2,1,0:T(8,128)(2,1)S(1)}, bf16[4,2,32,32,128]{4,3,2,1,0:T(8,128)(2,1)}, u32[]{:S(2)}) copy-start(bf16[4,2,32,32,128]{4,3,2,1,0:T(8,128)(2,1)} %param.10) | copy-start | bytes 6291460
  7.2 192.8 %all-reduce.9.cloned.1.call-start = ((), (), s32[]{:S(2)}) async-start(), calls=%async_computation | async-start | bytes 1572864 | tf_op jit(solution)/shard_map/psum | solution.py:141
  10.4 11.6 %collective-permute-start = (bf16[2,1,128,128]{3,0,2,1:T(2,128)(2,1)S(1)}, bf16[2,1,128,128]{3,0,2,1:T(2,128)(2,1)S(1)}, u32[]{:S(2)}, u32[]{:S(2)}) collective-permute-start(bf16[2,1,128,128]{3,0,2,1:T(2,128)(2,1)S(1)} %copy.17), channel_id=1, source_target_pairs={{0,1},{1,2},{2,3},{3,4},{4,5},{5,6},{6,7},{7,8},{8,9},{9,10},{10,1... | collective-permute-start | bytes 196616 | tf_op jit(solution)/shard_map/ppermute | solution.py:17
  13.5 9.3 %collective-permute-start.1 = (bf16[2,1,128,128]{3,0,2,1:T(2,128)(2,1)S(1)}, bf16[2,1,128,128]{3,0,2,1:T(2,128)(2,1)S(1)}, u32[]{:S(2)}, u32[]{:S(2)}) collective-permute-start(bf16[2,1,128,128]{3,0,2,1:T(2,128)(2,1)S(1)} %copy.22), channel_id=1, source_target_pairs={{1,0},{2,1},{3,2},{4,3},{5,4},{6,5},{7,6},{8,7},{9,8},{10,9},{11,1... | collective-permute-start | bytes 196616 | tf_op jit(solution)/shard_map/ppermute | solution.py:18
  17.0 5.8 %copy-start.6 = (s32[1024]{0:T(1024)}, s32[1024]{0:T(1024)S(1)}, u32[]{:S(2)}) copy-start(s32[1024]{0:T(1024)S(1)} %get-tuple-element.235) | copy-start | bytes 12292
  20.7 5.9 %copy-start.4 = (bf16[9,128,128]{2,1,0:T(8,128)(2,1)S(1)}, bf16[9,128,128]{2,1,0:T(8,128)(2,1)}, u32[]{:S(2)}) copy-start(bf16[9,128,128]{2,1,0:T(8,128)(2,1)} %param.13) | copy-start | bytes 884740
  28.5 1.9 copy-start.7
  31.8 2.0 copy-start.5
  37.0 0.5 copy-start.8
  37.0 74.7 %copy-start = (f32[1152,128]{1,0:T(8,128)}, f32[1152,128]{1,0:T(8,128)S(1)}, u32[]{:S(2)}) copy-start(f32[1152,128]{1,0:T(8,128)S(1)} %get-tuple-element.177) | copy-start | bytes 1769476
  37.0 74.7 %copy-start.3 = (f32[384,128]{1,0:T(8,128)}, f32[384,128]{1,0:T(8,128)S(1)}, u32[]{:S(2)}) copy-start(f32[384,128]{1,0:T(8,128)S(1)} %get-tuple-element.178) | copy-start | bytes 589828
  39.7 72.0 %collective-permute-start.2 = (bf16[2,1,128,128]{3,0,2,1:T(2,128)(2,1)}, bf16[2,1,128,128]{3,0,2,1:T(2,128)(2,1)}, u32[]{:S(2)}, u32[]{:S(2)}) collective-permute-start(bf16[2,1,128,128]{3,0,2,1:T(2,128)(2,1)} %copy.25), channel_id=1, source_target_pairs={{0,1},{1,2},{2,3},{3,4},{4,5},{5,6},{6,7},{7,8},{8,9},{9,10},{10,1... | collective-permute-start | bytes 196616 | tf_op jit(solution)/shard_map/ppermute | solution.py:17
  56.6 56.8 %collective-permute-start.3 = (bf16[2,1,128,128]{3,0,2,1:T(2,128)(2,1)}, bf16[2,1,128,128]{3,0,2,1:T(2,128)(2,1)}, u32[]{:S(2)}, u32[]{:S(2)}) collective-permute-start(bf16[2,1,128,128]{3,0,2,1:T(2,128)(2,1)} %copy.30), channel_id=1, source_target_pairs={{1,0},{2,1},{3,2},{4,3},{5,4},{6,5},{7,6},{8,7},{9,8},{10,9},{11,1... | collective-permute-start | bytes 196616 | tf_op jit(solution)/shard_map/ppermute | solution.py:18
  123.8 79.8 %copy-start.2 = (bf16[4,2,32,32,128]{4,3,2,1,0:T(8,128)(2,1)}, bf16[4,2,32,32,128]{4,3,2,1,0:T(8,128)(2,1)S(1)}, u32[]{:S(2)}) copy-start(bf16[4,2,32,32,128]{4,3,2,1,0:T(8,128)(2,1)S(1)} %get-tuple-element.171) | copy-start | bytes 6291460
Sparse Core Ops, SparseCore 0:
  111.9 88.0 all-reduce.8
where the time goes:
time: 211 us; the launch traced here: 210 us
  waiting for transfers between devices  76.2 us (36%)
  blocking collectives  50.5 us (24%)
  local copies, waits for them, and re-layouts  29.2 us (14%)
  starting transfers between devices  20.4 us (10%)
  between operations  14.5 us (7%)
  other arithmetic  11.2 us (5%)
  matrix products  5.68 us (3%)
  loops' own time  2.7 us (1%)
    psum x1, waiting for transfers between devices, per_device(): totals = lax.psum(partial_value, 'strip')  76.2 us
    psum x1, blocking collectives, per_device(): totals = lax.psum(partial_value, 'strip')  50.5 us
    ppermute x2, starting transfers between devices, padded_2(): before = lax.ppermute(last, axis, up)  17.8 us
    concatenate x2, other arithmetic, surround_tiles(): jnp.concatenate([top_rows[:, :, None], middle, bottom_rows[:, :, None]],...  5.29 us
  transfers between devices with their start and end apart: 5, of which 1 were waited for; matrix products, arithmetic and copies ran while one was open for 11% of the time, Pallas kernels for 0%

commit v1 on v0

v1 whole, which is shorter than its diff:
```python
import functools

import jax
import jax.numpy as jnp
from jax import lax
from jax.experimental import pallas as pl
from jax.experimental.pallas import tpu as pltpu
from jax.sharding import PartitionSpec as P

MESH = pl.DeviceIdType.MESH
F32, BF16 = jnp.float32, jnp.bfloat16
PAIRS = 8


def radices_of(size):
    found, rest = [], size
    for radix in (2, 2):
        if rest % radix == 0:
            found.append(radix)
            rest //= radix
    while rest % 4 == 0:
        found.append(4)
        rest //= 4
    if rest > 1:
        found.append(rest)
    return found


def dot_rows(a, b):
    return lax.dot_general(a, b, (((0,), (0,)), ((), ())), preferred_element_type=F32)


def kernel(size, radices, chunk, scale, x_ref, g_ref, pos_ref, ws_ref, bias_ref, wt_ref,
           out_ref, ds_ref, dt_ref, db_ref,
           wf, wb, wtt, x3, gp, gpa, ha, ga, psum, tsum, bsum, edge_x, edge_g, halo_x, halo_g,
           acc, send, total, *rest):
    n_st = len(radices)
    landing = rest[:n_st]
    esend, erecv, gsend, grecv, rsend, rrecv, asend, arecv = rest[n_st:]
    slots, frames, half, _, width, ch = x_ref.shape
    wide = 3 * ch
    me = lax.axis_index("strip")

    strides, digits, partners = [], [], []
    stride = 1
    for radix in radices:
        digit = lax.rem(me // stride, radix)
        strides.append(stride)
        digits.append(digit)
        partners.append([me + (lax.rem(digit + d, radix) - digit) * stride for d in range(1, radix)])
        stride *= radix

    barrier = pltpu.get_barrier_semaphore()
    greeted = [lax.rem(me + 1, size), lax.rem(me + size - 1, size)]
    for stage in partners:
        greeted += stage
    for other in greeted:
        pl.semaphore_signal(barrier, inc=1, device_id={"strip": other}, device_id_type=MESH)

    def slot_of(c):
        slot, act = jnp.int32(0), jnp.int32(0)
        for s in range(slots):
            hit = (pos_ref[s] == c) & (c >= 0)
            slot = jnp.where(hit, s, slot)
            act = jnp.where(hit, 1, act)
        return slot, act.astype(F32)

    def edge_copies(edge, halo, ssem, rsem):
        up = pltpu.make_async_remote_copy(
            src_ref=edge.at[0], dst_ref=halo.at[1], send_sem=ssem.at[0], recv_sem=rsem.at[1],
            device_id={"strip": jnp.maximum(me - 1, 0)}, device_id_type=MESH)
        down = pltpu.make_async_remote_copy(
            src_ref=edge.at[1], dst_ref=halo.at[0], send_sem=ssem.at[1], recv_sem=rsem.at[0],
            device_id={"strip": jnp.minimum(me + 1, size - 1)}, device_id_type=MESH)
        return up, down

    def edge_start(copies):
        up, down = copies

        @pl.when(me > 0)
        def _():
            up.start()

        @pl.when(me < size - 1)
        def _():
            down.start()

    def edge_wait(copies):
        up, down = copies

        @pl.when(me > 0)
        def _():
            up.wait_send()
            down.wait_recv()

        @pl.when(me < size - 1)
        def _():
            down.wait_send()
            up.wait_recv()

    for halo in (halo_x, halo_g):
        @pl.when(me == 0)
        def _():
            halo[0] = jnp.zeros_like(halo[0])

        @pl.when(me == size - 1)
        def _():
            halo[1] = jnp.zeros_like(halo[1])

    for c in range(slots):
        slot, act = slot_of(c)
        for f in range(frames):
            edge_x[0, c, f] = (x_ref[slot, f, 0, 0].astype(F32) * act).astype(BF16)
            edge_x[1, c, f] = (x_ref[slot, f, half - 1, 1].astype(F32) * act).astype(BF16)
    pl.semaphore_wait(barrier, len(greeted))
    x_copies = edge_copies(edge_x, halo_x, esend, erecv)
    edge_start(x_copies)

    zero = jnp.zeros((ch, ch), BF16)
    for r in range(4):
        for b in range(3):
            rows = pl.ds((r * 3 + b) * ch, ch)
            wf[rows, :ch] = ws_ref[3 * r + b] if r < 3 else zero
            wf[rows, ch:] = ws_ref[3 * (r - 1) + b] if r > 0 else zero
            if r == 3:
                wb[rows, :ch] = zero
            if r == 0:
                wb[rows, ch:] = zero
            if r < 3:
                turned = ws_ref[3 * (2 - r) + 2 - b].astype(F32).T.astype(BF16)
                wb[rows, :ch] = turned
                wb[pl.ds(((r + 1) * 3 + b) * ch, ch), ch:] = turned
    for row, col, k in ((0, 0, 1), (0, 1, 2), (1, 0, 0), (1, 1, 1)):
        wtt[row * ch:(row + 1) * ch, col * ch:(col + 1) * ch] = wt_ref[k].astype(F32).T.astype(BF16)
    psum[...] = jnp.zeros_like(psum)
    tsum[...] = jnp.zeros_like(tsum)
    bsum[...] = jnp.zeros_like(bsum)
    bias_pair = jnp.concatenate([bias_ref[...], bias_ref[...]], axis=1)

    column = lax.broadcasted_iota(jnp.int32, (1, width, 1), 1)

    def put(f, q, t, center, left, right):
        mid = center.astype(F32)
        before = jnp.where(column == 0, left, pltpu.roll(mid, 1, 1))
        after = jnp.where(column == width - 1, right, pltpu.roll(mid, width - 1, 1))
        x3[f, q, t, :, :ch] = before.astype(BF16)
        x3[f, q, t, :, ch:2 * ch] = center
        x3[f, q, t, :, 2 * ch:] = after.astype(BF16)

    def last_col(values, keep):
        return values.astype(F32)[:, -1:, :] * keep

    def first_col(values, keep):
        return values.astype(F32)[:, :1, :] * keep

    tail = slice(width - 16, width)
    head = slice(0, 16)

    def put_halo(halo, c, left_keep, right_keep):
        lc, rc = jnp.maximum(c - 1, 0), jnp.minimum(c + 1, slots - 1)
        for side, q, t in ((0, 0, 0), (1, half, 1)):
            for f in range(frames):
                put(f, pl.ds(q, 1), t, halo[side, pl.ds(c, 1), f],
                    last_col(halo[side, pl.ds(lc, 1), f, tail], left_keep),
                    first_col(halo[side, pl.ds(rc, 1), f, head], right_keep))

    def taps(f, m, r):
        part = x3[f, pl.ds(m + r // 2, PAIRS), r % 2]
        return part.reshape(PAIRS * width, wide)

    def four(f, m):
        return jnp.concatenate([taps(f, m, r) for r in range(4)], axis=1)

    span = PAIRS * width
    steps = half // PAIRS

    edge_wait(x_copies)

    def first(c, carry):
        slot, act = slot_of(c)
        lslot, lact = slot_of(c - 1)
        rslot, ract = slot_of(c + 1)
        inner_l = (c > 0).astype(F32)
        inner_r = (c < slots - 1).astype(F32)
        put_halo(halo_x, c, inner_l, inner_r)

        def build(i, carry):
            m = i * PAIRS
            for f in range(frames):
                for t in range(2):
                    rows = pl.ds(m, PAIRS)
                    put(f, pl.ds(m + t, PAIRS), 1 - t, x_ref[slot, f, rows, t],
                        last_col(x_ref[lslot, f, rows, t, tail], lact),
                        first_col(x_ref[rslot, f, rows, t, head], ract))
            return carry

        lax.fori_loop(0, steps, build, 0)

        def advance(i, carry):
            m = i * PAIRS
            rows = pl.ds(m, PAIRS)
            grads, hid = [], []
            for t in range(2):
                both = [g_ref[slot, f, rows, t].reshape(span, ch) for f in range(frames)]
                pair = jnp.concatenate(both, axis=1)
                ga[pl.ds((2 * i + t) * span, span), :] = pair
                grads.append(jnp.dot(pair, wtt[...], preferred_element_type=F32))
            for f in range(frames):
                pre = jnp.dot(four(f, m), wf[...], preferred_element_type=F32) + bias_pair
                sig = 0.5 * jnp.tanh(0.5 * pre) + 0.5
                hidden = pre * sig
                slope = sig + hidden * (1.0 - sig)
                gh = jnp.concatenate([grads[0][:, f * ch:(f + 1) * ch], grads[1][:, f * ch:(f + 1) * ch]], axis=1)
                gpre = (gh * (slope * act)).astype(BF16)
                hid_b = (hidden * act).astype(BF16)
                for t in range(2):
                    ha[pl.ds((2 * i + t) * span, span), f * ch:(f + 1) * ch] = hid_b[:, t * ch:(t + 1) * ch]
                    gp[c, f, pl.ds(m + t, PAIRS), 1 - t] = gpre[:, t * ch:(t + 1) * ch].reshape(PAIRS, width, ch)
                gpa[pl.ds((f * steps + i) * span, span), :] = gpre
                wide_g = gpre.astype(F32).reshape(span // 8, 8, 2 * ch)
                bsum[...] += jnp.sum(wide_g, axis=0)
            return carry

        lax.fori_loop(0, steps, advance, 0)
        tsum[...] += dot_rows(ha[...], ga[...])
        gpv = gpa[...]
        for r in range(4):
            cells = x3[:, pl.ds(r // 2, half), r % 2].reshape(frames * half * width, wide)
            psum[r] += dot_rows(gpv, cells)
        return carry

    lax.fori_loop(0, slots, first, 0)

    for c in range(slots):
        for f in range(frames):
            edge_g[0, c, f] = gp[c, f, 0, 1]
            edge_g[1, c, f] = gp[c, f, half, 0]
    g_copies = edge_copies(edge_g, halo_g, gsend, grecv)
    edge_start(g_copies)

    for a in range(3):
        for b in range(3):
            cols = slice(b * ch, (b + 1) * ch)
            block = psum[a, :ch, cols] + psum[a + 1, ch:, cols]
            acc[pl.ds((3 * a + b) * ch, ch), :] = block.T
    base = 9 * ch
    acc[base:base + ch, :] = tsum[:ch, ch:]
    acc[base + ch:base + 2 * ch, :] = tsum[:ch, :ch] + tsum[ch:, ch:]
    acc[base + 2 * ch:base + 3 * ch, :] = tsum[ch:, :ch]
    base = 12 * ch
    acc[base:, :] = jnp.zeros_like(acc[base:, :])
    acc[base:base + 8, :] = bsum[:, :ch] + bsum[:, ch:]

    lows, parts = [], []
    low, part = 0, size * chunk
    for radix, digit in zip(radices, digits):
        part //= radix
        lows.append(low)
        parts.append(part)
        low = low + digit * part
    own = low

    def at(offset, rows):
        return pl.ds(pl.multiple_of(offset, 16), rows)

    started = []

    def scatter_copy(k, d):
        radix, part = radices[k], parts[k]
        target = lax.rem(digits[k] + d, radix)
        return pltpu.make_async_remote_copy(
            src_ref=send.at[at(lows[k] + target * part, part)], dst_ref=landing[k].at[d - 1],
            send_sem=rsend.at[k, d], recv_sem=rrecv.at[k, d],
            device_id={"strip": partners[k][d - 1]}, device_id_type=MESH)

    def scatter_start(k):
        part = parts[k]
        for d in range(1, radices[k]):
            target = lax.rem(digits[k] + d, radices[k])
            rows = at(lows[k] + target * part, part)
            send[rows, :] = acc[rows, :].astype(BF16)
            copy = scatter_copy(k, d)
            copy.start()
            started.append(copy)

    def scatter_finish(k):
        rows = at(lows[k] + digits[k] * parts[k], parts[k])
        for d in range(1, radices[k]):
            scatter_copy(k, d).wait_recv()
        got = acc[rows, :]
        for d in range(1, radices[k]):
            got = got + landing[k][d - 1].astype(F32)
        acc[rows, :] = got

    def gather_copy(k, d, back):
        part = parts[k]
        digit = lax.rem(digits[k] + radices[k] - d, radices[k]) if back else digits[k]
        rows = at(lows[k] + digit * part, part)
        return pltpu.make_async_remote_copy(
            src_ref=total.at[rows], dst_ref=total.at[rows],
            send_sem=asend.at[k, d], recv_sem=arecv.at[k, d],
            device_id={"strip": partners[k][d - 1]}, device_id_type=MESH)

    def gather_start(k):
        for d in range(1, radices[k]):
            copy = gather_copy(k, d, False)
            copy.start()
            started.append(copy)

    def gather_finish(k):
        for d in range(1, radices[k]):
            gather_copy(k, d, True).wait_recv()

    work = [functools.partial(scatter_start, 0)]
    for k in range(n_st):
        def hop(k=k):
            scatter_finish(k)
            if k + 1 < n_st:
                scatter_start(k + 1)
            else:
                rows = at(own, chunk)
                total[rows, :] = acc[rows, :].astype(BF16)
                gather_start(n_st - 1)
        work.append(hop)
    for k in reversed(range(n_st)):
        def back(k=k):
            gather_finish(k)
            if k > 0:
                gather_start(k - 1)
        work.append(back)

    work.pop(0)()
    edge_wait(g_copies)

    for s in range(slots):
        c = jnp.maximum(pos_ref[s], 0)
        act = (pos_ref[s] >= 0).astype(F32)
        inner_l = (c > 0).astype(F32)
        inner_r = (c < slots - 1).astype(F32)
        lc, rc = jnp.maximum(c - 1, 0), jnp.minimum(c + 1, slots - 1)
        put_halo(halo_g, c, inner_l, inner_r)

        def build(i, carry):
            m = i * PAIRS
            for f in range(frames):
                for t in range(2):
                    q = pl.ds(m + t, PAIRS)
                    put(f, q, 1 - t, gp[c, f, q, 1 - t],
                        last_col(gp[lc, f, q, 1 - t, tail], inner_l),
                        first_col(gp[rc, f, q, 1 - t, head], inner_r))
            return carry

        lax.fori_loop(0, steps, build, 0)

        def second(i, carry):
            m = i * PAIRS
            for f in range(frames):
                res = (jnp.dot(four(f, m), wb[...], preferred_element_type=F32) * act).astype(BF16)
                for t in range(2):
                    out_ref[s, f, pl.ds(m, PAIRS), t] = res[:, t * ch:(t + 1) * ch].reshape(PAIRS, width, ch)
            return carry

        lax.fori_loop(0, steps, second, 0)
        work.pop(0)()
    while work:
        work.pop(0)()

    for tap in range(9):
        ds_ref[tap] = total[tap * ch:(tap + 1) * ch, :].astype(F32) * scale
    for tap in range(3):
        dt_ref[tap] = total[(9 + tap) * ch:(10 + tap) * ch, :].astype(F32) * scale
    base = 12 * ch
    rows = total[base:base + 16, :].astype(F32)
    db_ref[...] = jnp.sum(rows, axis=0, keepdims=True) * scale
    for copy in started:
        copy.wait_send()


def per_device(size, x_tiles, grad_out, tile_pos, w_spatial, conv_bias, w_temporal):
    slots, frames, height, width, ch = x_tiles.shape
    half = height // 2
    radices = radices_of(size)
    rows = 12 * ch + 16
    chunk = -(-rows // (size * 16)) * 16
    full = chunk * size
    scale = float(size * slots * frames * height * height) ** -0.5
    cells = frames * half * width
    paired = (slots, frames, half, 2, width, ch)
    edge = (2, slots, frames, width, ch)
    landing, part = [], full
    for radix in radices:
        part //= radix
        landing.append(pltpu.VMEM((radix - 1, part, ch), BF16))
    most = max(radices)
    vmem = pl.BlockSpec(memory_space=pltpu.VMEM)
    smem = pl.BlockSpec(memory_space=pltpu.SMEM)
    grad_in, d_spatial, d_temporal, d_bias = pl.pallas_call(
        functools.partial(kernel, size, radices, chunk, scale),
        out_shape=(
            jax.ShapeDtypeStruct(paired, BF16),
            jax.ShapeDtypeStruct((9, ch, ch), F32),
            jax.ShapeDtypeStruct((3, ch, ch), F32),
            jax.ShapeDtypeStruct((1, ch), F32),
        ),
        in_specs=[vmem, vmem, smem, vmem, vmem, vmem],
        out_specs=(vmem, vmem, vmem, vmem),
        scratch_shapes=[
            pltpu.VMEM((12 * ch, 2 * ch), BF16),
            pltpu.VMEM((12 * ch, 2 * ch), BF16),
            pltpu.VMEM((2 * ch, 2 * ch), BF16),
            pltpu.VMEM((frames, half + 1, 2, width, 3 * ch), BF16),
            pltpu.VMEM((slots, frames, half + 1, 2, width, ch), BF16),
            pltpu.VMEM((cells, 2 * ch), BF16),
            pltpu.VMEM((cells, 2 * ch), BF16),
            pltpu.VMEM((cells, 2 * ch), BF16),
            pltpu.VMEM((4, 2 * ch, 3 * ch), F32),
            pltpu.VMEM((2 * ch, 2 * ch), F32),
            pltpu.VMEM((8, 2 * ch), F32),
            pltpu.VMEM(edge, BF16),
            pltpu.VMEM(edge, BF16),
            pltpu.VMEM(edge, BF16),
            pltpu.VMEM(edge, BF16),
            pltpu.VMEM((full, ch), F32),
            pltpu.VMEM((full, ch), BF16),
            pltpu.VMEM((full, ch), BF16),
            *landing,
            pltpu.SemaphoreType.DMA((2,)),
            pltpu.SemaphoreType.DMA((2,)),
            pltpu.SemaphoreType.DMA((2,)),
            pltpu.SemaphoreType.DMA((2,)),
            pltpu.SemaphoreType.DMA((len(radices), most)),
            pltpu.SemaphoreType.DMA((len(radices), most)),
            pltpu.SemaphoreType.DMA((len(radices), most)),
            pltpu.SemaphoreType.DMA((len(radices), most)),
        ],
        compiler_params=pltpu.CompilerParams(
            collective_id=0, has_side_effects=True, vmem_limit_bytes=48 * 2**20
        ),
    )(
        x_tiles.reshape(paired),
        grad_out.reshape(paired),
        tile_pos,
        w_spatial,
        conv_bias.reshape(1, ch),
        w_temporal,
    )
    return grad_in.reshape(x_tiles.shape), d_spatial, d_temporal, d_bias.reshape(ch)


def solution(mesh):
    tiles = P(("groups", "strip"), None, None, None, None)
    in_specs = (tiles, tiles, P(("groups", "strip")), P(), P(), P())
    out_specs = (tiles, P("groups", None, None), P("groups", None, None), P("groups"))
    return jax.shard_map(
        functools.partial(per_device, mesh.shape["strip"]),
        mesh=mesh, in_specs=in_specs, out_specs=out_specs, check_vma=False,
    )
```

time: 211 us -> 56 us (0.27)
  waiting for transfers between devices: 76.2 us -> 0 us
  blocking collectives: 50.5 us -> 0 us
  Pallas kernels: 0 us -> 47 us
  local copies, waits for them, and re-layouts: 29.2 us -> 8.07 us
  starting transfers between devices: 20.4 us -> 0 us
  between operations: 14.5 us -> 0.65 us
  other arithmetic: 11.2 us -> 0 us
  matrix products: 5.68 us -> 0 us
  loops' own time: 2.7 us -> 0 us
    psum x1 -> x0, waiting for transfers between devices: 76.2 us -> none  [per_device(): totals = lax.psum(partial_value, 'strip')]
    psum x1 -> x0, blocking collectives: 50.5 us -> none  [per_device(): totals = lax.psum(partial_value, 'strip')]
    pallas_call x0 -> x1, Pallas kernels: none -> 47 us  [per_device(): pl.pallas_call(functools.partial(kernel, size, radices, chunk, scale), ou...]
    ppermute x4 -> x0, starting transfers between devices: 20.4 us -> none  [the longest x2 17.8 us: padded_2(): before = lax.ppermute(last, axis, up)]
    unnamed x14, local copies, waits for them, and re-layouts: 0.51 us -> 8.07 us
    dot_general x5 -> x0, matrix products: 5.68 us -> none  [the longest x1 1.49 us: backward_terms(): jnp.dot(columns.T, grad_pre, preferred_element_type=jnp.float32)]
    concatenate x2 -> x0, other arithmetic: 5.29 us -> none  [surround_tiles(): jnp.concatenate([top_rows[:, :, None], middle, bottom_rows[:, :, None]],...]
    scatter x8 -> x0, local copies, waits for them, and re-layouts: 5.25 us -> none  [the longest x4 2.65 us: dense_row(): jnp.zeros(edge_cells.shape, edge_cells.dtype).at[:, target]]
  transfers between devices with their start and end apart: 5 -> 0, of which waited for: 1 -> 0; matrix products, arithmetic and copies ran while one was open for 11% -> 0% of each run, Pallas kernels for 0% -> 0%
where the time goes in v1:
time: 56 us; the launch traced here: 55.7 us
  Pallas kernels  47 us (84%)
  local copies, waits for them, and re-layouts  8.07 us (14%)
  between operations  0.65 us (1%)
    pallas_call x1, Pallas kernels, per_device(): pl.pallas_call(functools.partial(kernel, size, radices, chunk, scale), ou...  47 us
    unnamed x14, local copies, waits for them, and re-layouts  8.07 us

profile of v1, /device:TPU:0, one launch (start us, length us, event | category | flops | bytes accessed | tf_op | source)
XLA Modules:
  0.0 55.7 jit_solution(7093356522670641818)
XLA Ops:
  0.6 0.0 copy-start
  0.6 1.6 %copy-done = bf16[4,2,32,32,128]{4,3,2,1,0:T(8,128)(2,1)S(1)} copy-done((bf16[4,2,32,32,128]{4,3,2,1,0:T(8,128)(2,1)S(1)}, bf16[4,2,32,32,128]{4,3,2,1,0:T(8,128)(2,1)}, u32[]{:S(2)}) %copy-start) | copy-done | bytes 2097176
  2.2 0.0 copy-start.1
  2.2 1.0 %copy-done.1 = bf16[9,128,128]{2,1,0:T(8,128)(2,1)S(1)} copy-done((bf16[9,128,128]{2,1,0:T(8,128)(2,1)S(1)}, bf16[9,128,128]{2,1,0:T(8,128)(2,1)}, u32[]{:S(2)}) %copy-start.1) | copy-done | bytes 294936
  3.2 0.0 copy-start.2
  3.2 0.9 %copy-done.2 = bf16[3,128,128]{2,1,0:T(8,128)(2,1)S(1)} copy-done((bf16[3,128,128]{2,1,0:T(8,128)(2,1)S(1)}, bf16[3,128,128]{2,1,0:T(8,128)(2,1)}, u32[]{:S(2)}) %copy-start.2) | copy-done | bytes 98328
  4.1 0.0 copy-start.3
  4.1 0.7 %copy-done.3 = s32[4]{0:T(128)S(1)} copy-done((s32[4]{0:T(128)S(1)}, s32[4]{0:T(128)}, u32[]{:S(2)}) %copy-start.3) | copy-done | bytes 40
  4.7 0.0 copy-start.4
  4.7 0.7 %copy-done.4 = f32[128]{0:T(128)S(1)} copy-done((f32[128]{0:T(128)S(1)}, f32[128]{0:T(128)}, u32[]{:S(2)}) %copy-start.4) | copy-done | bytes 536
  5.4 47.0 %shard_map.93 = (bf16[4,2,16,2,32,128]{5,4,3,2,1,0:T(8,128)(2,1)S(1)}, f32[9,128,128]{2,1,0:T(8,128)S(1)}, f32[3,128,128]{2,1,0:T(8,128)S(1)}, f32[1,128]{1,0:T(1,128)S(1)}) custom-call(bf16[4,2,16,2,32,128]{5,4,3,2,1,0:T(8,128)(2,1)S(1)} %bitcast.5, bf16[4,2,16,2,32,128]{5,4,3,2,1,0:T(8,128)(2,1)} %bitcast.9, s32[4]{0:T(128)S(1)} %copy-done.3, ...), custom_call_target="tpu_custom_call" | custom-call | tf_op jit(solution)/shard_map/pallas_call | solution.py:397
  52.4 1.3 %copy.14 = bf16[4,2,32,32,128]{4,3,2,1,0:T(8,128)(2,1)} copy(bf16[4,2,32,32,128]{4,3,2,1,0:T(8,128)(2,1)S(1)} %bitcast.6) | data formatting | bytes 4194304
  53.7 0.8 %copy.15 = f32[9,128,128]{2,1,0:T(8,128)} copy(f32[9,128,128]{2,1,0:T(8,128)S(1)} %get-tuple-element.17) | data formatting | bytes 1179648
  54.5 0.7 %copy.16 = f32[3,128,128]{2,1,0:T(8,128)} copy(f32[3,128,128]{2,1,0:T(8,128)S(1)} %get-tuple-element.18) | data formatting | bytes 393216
  55.2 0.5 copy.17
Async XLA Ops:
  0.6 1.6 %copy-start = (bf16[4,2,32,32,128]{4,3,2,1,0:T(8,128)(2,1)S(1)}, bf16[4,2,32,32,128]{4,3,2,1,0:T(8,128)(2,1)}, u32[]{:S(2)}) copy-start(bf16[4,2,32,32,128]{4,3,2,1,0:T(8,128)(2,1)} %param.6) | copy-start | bytes 6291460
  2.2 1.0 %copy-start.1 = (bf16[9,128,128]{2,1,0:T(8,128)(2,1)S(1)}, bf16[9,128,128]{2,1,0:T(8,128)(2,1)}, u32[]{:S(2)}) copy-start(bf16[9,128,128]{2,1,0:T(8,128)(2,1)} %ws_ref.1) | copy-start | bytes 884740
  3.2 0.9 %copy-start.2 = (bf16[3,128,128]{2,1,0:T(8,128)(2,1)S(1)}, bf16[3,128,128]{2,1,0:T(8,128)(2,1)}, u32[]{:S(2)}) copy-start(bf16[3,128,128]{2,1,0:T(8,128)(2,1)} %wt_ref.1) | copy-start | bytes 294916
  4.1 0.7 %copy-start.3 = (s32[4]{0:T(128)S(1)}, s32[4]{0:T(128)}, u32[]{:S(2)}) copy-start(s32[4]{0:T(128)} %pos_ref.1) | copy-start | bytes 52
  4.7 0.7 %copy-start.4 = (f32[128]{0:T(128)S(1)}, f32[128]{0:T(128)}, u32[]{:S(2)}) copy-start(f32[128]{0:T(128)} %param.10) | copy-start | bytes 1540

commit v2 on v1

v2 whole, which is shorter than its diff:
```python
import functools

import jax
import jax.numpy as jnp
from jax import lax
from jax.experimental import pallas as pl
from jax.experimental.pallas import tpu as pltpu
from jax.sharding import PartitionSpec as P

MESH = pl.DeviceIdType.MESH
F32, BF16 = jnp.float32, jnp.bfloat16
PAIRS = 8


def radices_of(size):
    found, rest = [], size
    for radix in (2, 2):
        if rest % radix == 0:
            found.append(radix)
            rest //= radix
    while rest % 4 == 0:
        found.append(4)
        rest //= 4
    if rest > 1:
        found.append(rest)
    return found


def dot_rows(a, b):
    return lax.dot_general(a, b, (((0,), (0,)), ((), ())), preferred_element_type=F32)


def kernel(size, radices, chunk, x_hbm, g_hbm, pos_ref, ws_hbm, bias_hbm, wt_hbm,
           out_ref, tot_ref, db_ref,
           x_ref, g_ref, ws_ref, bias_ref, wt_ref, in_sem, wf, wb, wtt, x3, gp, gpa, ha, ga, psum, tsum, bsum, edge_x, edge_g, halo_x, halo_g,
           acc, send, total, bstage, *rest):
    n_st = len(radices)
    landing, blanding = rest[:n_st], rest[n_st:2 * n_st]
    esend, erecv, gsend, grecv, rsend, rrecv, asend, arecv, bsend, brecv = rest[2 * n_st:]
    loads = [
        pltpu.make_async_copy(src, dst, in_sem.at[i])
        for i, (src, dst) in enumerate(
            ((x_hbm, x_ref), (ws_hbm, ws_ref), (g_hbm, g_ref), (wt_hbm, wt_ref), (bias_hbm, bias_ref)))
    ]
    for load in loads:
        load.start()
    slots, frames, half, _, width, ch = x_ref.shape
    wide = 3 * ch
    me = lax.axis_index("strip")

    strides, digits, partners = [], [], []
    stride = 1
    for radix in radices:
        digit = lax.rem(me // stride, radix)
        strides.append(stride)
        digits.append(digit)
        partners.append([me + (lax.rem(digit + d, radix) - digit) * stride for d in range(1, radix)])
        stride *= radix

    barrier = pltpu.get_barrier_semaphore()
    greeted = [lax.rem(me + 1, size), lax.rem(me + size - 1, size)]
    for stage in partners:
        greeted += stage
    for other in greeted:
        pl.semaphore_signal(barrier, inc=1, device_id={"strip": other}, device_id_type=MESH)

    def slot_of(c):
        slot, act = jnp.int32(0), jnp.int32(0)
        for s in range(slots):
            hit = (pos_ref[s] == c) & (c >= 0)
            slot = jnp.where(hit, s, slot)
            act = jnp.where(hit, 1, act)
        return slot, act.astype(F32)

    def edge_copies(edge, halo, ssem, rsem):
        up = pltpu.make_async_remote_copy(
            src_ref=edge.at[0], dst_ref=halo.at[1], send_sem=ssem.at[0], recv_sem=rsem.at[1],
            device_id={"strip": jnp.maximum(me - 1, 0)}, device_id_type=MESH)
        down = pltpu.make_async_remote_copy(
            src_ref=edge.at[1], dst_ref=halo.at[0], send_sem=ssem.at[1], recv_sem=rsem.at[0],
            device_id={"strip": jnp.minimum(me + 1, size - 1)}, device_id_type=MESH)
        return up, down

    def edge_start(copies):
        up, down = copies

        @pl.when(me > 0)
        def _():
            up.start()

        @pl.when(me < size - 1)
        def _():
            down.start()

    def edge_wait(copies):
        up, down = copies

        @pl.when(me > 0)
        def _():
            up.wait_send()
            down.wait_recv()

        @pl.when(me < size - 1)
        def _():
            down.wait_send()
            up.wait_recv()

    for halo in (halo_x, halo_g):
        @pl.when(me == 0)
        def _():
            halo[0] = jnp.zeros_like(halo[0])

        @pl.when(me == size - 1)
        def _():
            halo[1] = jnp.zeros_like(halo[1])

    loads[0].wait()
    for c in range(slots):
        slot, act = slot_of(c)
        for f in range(frames):
            edge_x[0, c, f] = (x_ref[slot, f, 0, 0].astype(F32) * act).astype(BF16)
            edge_x[1, c, f] = (x_ref[slot, f, half - 1, 1].astype(F32) * act).astype(BF16)
    pl.semaphore_wait(barrier, len(greeted))
    x_copies = edge_copies(edge_x, halo_x, esend, erecv)
    edge_start(x_copies)

    loads[1].wait()
    loads[3].wait()
    loads[4].wait()
    zero = jnp.zeros((ch, ch), BF16)
    for r in range(4):
        for b in range(3):
            rows = pl.ds((r * 3 + b) * ch, ch)
            wf[rows, :ch] = ws_ref[3 * r + b] if r < 3 else zero
            wf[rows, ch:] = ws_ref[3 * (r - 1) + b] if r > 0 else zero
            if r == 3:
                wb[rows, :ch] = zero
            if r == 0:
                wb[rows, ch:] = zero
            if r < 3:
                turned = ws_ref[3 * (2 - r) + 2 - b].astype(F32).T.astype(BF16)
                wb[rows, :ch] = turned
                wb[pl.ds(((r + 1) * 3 + b) * ch, ch), ch:] = turned
    for row, col, k in ((0, 0, 1), (0, 1, 2), (1, 0, 0), (1, 1, 1)):
        wtt[row * ch:(row + 1) * ch, col * ch:(col + 1) * ch] = wt_ref[k].astype(F32).T.astype(BF16)
    psum[...] = jnp.zeros_like(psum)
    tsum[...] = jnp.zeros_like(tsum)
    bsum[...] = jnp.zeros_like(bsum)
    bias_pair = jnp.concatenate([bias_ref[...], bias_ref[...]], axis=1)

    column = lax.broadcasted_iota(jnp.int32, (1, width, 1), 1)

    def put(n, f, q, t, center, left, right):
        mid = center.astype(F32)
        before = jnp.where(column == 0, left, pltpu.roll(mid, 1, 1))
        after = jnp.where(column == width - 1, right, pltpu.roll(mid, width - 1, 1))
        x3[n, f, q, t, :, :ch] = before.astype(BF16)
        x3[n, f, q, t, :, ch:2 * ch] = center
        x3[n, f, q, t, :, 2 * ch:] = after.astype(BF16)

    def last_col(values, keep):
        return values.astype(F32)[:, -1:, :] * keep

    def first_col(values, keep):
        return values.astype(F32)[:, :1, :] * keep

    tail = slice(width - 16, width)
    head = slice(0, 16)

    def put_halo(halo, n, c, left_keep, right_keep):
        lc, rc = jnp.maximum(c - 1, 0), jnp.minimum(c + 1, slots - 1)
        for side, q, t in ((0, 0, 0), (1, half, 1)):
            for f in range(frames):
                put(n, f, pl.ds(q, 1), t, halo[side, pl.ds(c, 1), f],
                    last_col(halo[side, pl.ds(lc, 1), f, tail], left_keep),
                    first_col(halo[side, pl.ds(rc, 1), f, head], right_keep))

    def taps(n, f, m, r):
        part = x3[n, f, pl.ds(m + r // 2, PAIRS), r % 2]
        return part.reshape(PAIRS * width, wide)

    def four(n, f, m):
        return jnp.concatenate([taps(n, f, m, r) for r in range(4)], axis=1)

    span = PAIRS * width
    steps = half // PAIRS

    edge_wait(x_copies)
    loads[2].wait()

    def first(c, carry):
        slot, act = slot_of(c)
        lslot, lact = slot_of(c - 1)
        rslot, ract = slot_of(c + 1)
        inner_l = (c > 0).astype(F32)
        inner_r = (c < slots - 1).astype(F32)
        put_halo(halo_x, c, c, inner_l, inner_r)

        def build(i, carry):
            m = i * PAIRS
            for f in range(frames):
                for t in range(2):
                    rows = pl.ds(m, PAIRS)
                    put(c, f, pl.ds(m + t, PAIRS), 1 - t, x_ref[slot, f, rows, t],
                        last_col(x_ref[lslot, f, rows, t, tail], lact),
                        first_col(x_ref[rslot, f, rows, t, head], ract))
            return carry

        lax.fori_loop(0, steps, build, 0)

        def advance(i, carry):
            m = i * PAIRS
            rows = pl.ds(m, PAIRS)
            grads, hid = [], []
            for t in range(2):
                both = [g_ref[slot, f, rows, t].reshape(span, ch) for f in range(frames)]
                pair = jnp.concatenate(both, axis=1)
                ga[pl.ds((2 * i + t) * span, span), :] = pair
                grads.append(jnp.dot(pair, wtt[...], preferred_element_type=F32))
            for f in range(frames):
                pre = jnp.dot(four(c, f, m), wf[...], preferred_element_type=F32) + bias_pair
                sig = 0.5 * jnp.tanh(0.5 * pre) + 0.5
                hidden = pre * sig
                slope = sig + hidden * (1.0 - sig)
                gh = jnp.concatenate([grads[0][:, f * ch:(f + 1) * ch], grads[1][:, f * ch:(f + 1) * ch]], axis=1)
                gpre = (gh * (slope * act)).astype(BF16)
                hid_b = (hidden * act).astype(BF16)
                for t in range(2):
                    ha[pl.ds((2 * i + t) * span, span), f * ch:(f + 1) * ch] = hid_b[:, t * ch:(t + 1) * ch]
                    gp[c, f, pl.ds(m + t, PAIRS), 1 - t] = gpre[:, t * ch:(t + 1) * ch].reshape(PAIRS, width, ch)
                gpa[c, pl.ds((f * steps + i) * span, span), :] = gpre
                wide_g = gpre.astype(F32).reshape(span // 8, 8, 2 * ch)
                bsum[...] += jnp.sum(wide_g, axis=0)
            return carry

        lax.fori_loop(0, steps, advance, 0)
        tsum[...] += dot_rows(ha[...], ga[...])
        return carry

    lax.fori_loop(0, slots, first, 0)

    for c in range(slots):
        for f in range(frames):
            edge_g[0, c, f] = gp[c, f, 0, 1]
            edge_g[1, c, f] = gp[c, f, half, 0]
    g_copies = edge_copies(edge_g, halo_g, gsend, grecv)
    edge_start(g_copies)

    def kernel_sums(taps_of):
        def add(c, carry):
            turned = gpa[c]
            for r in taps_of:
                cells = x3[c, :, pl.ds(r // 2, half), r % 2].reshape(frames * half * width, wide)
                psum[r] += dot_rows(turned, cells)
            return carry

        lax.fori_loop(0, slots, add, 0)

    def spread(piece, base, a):
        for b in range(3):
            cols = slice(b * ch, (b + 1) * ch)
            block = psum[a, :ch, cols] + psum[a + 1, ch:, cols]
            acc[piece, pl.ds(base + b * ch, ch), :] = block.T

    if size * chunk > 6 * ch:
        acc[:, 6 * ch:, :] = jnp.zeros_like(acc[:, 6 * ch:, :])
    acc[0, :ch, :] = tsum[:ch, ch:]
    acc[0, ch:2 * ch, :] = tsum[:ch, :ch] + tsum[ch:, ch:]
    acc[0, 2 * ch:3 * ch, :] = tsum[ch:, :ch]
    bstage[0] = bsum[:, :ch] + bsum[:, ch:]

    lows, parts = [], []
    low, part = 0, size * chunk
    for radix, digit in zip(radices, digits):
        part //= radix
        lows.append(low)
        parts.append(part)
        low = low + digit * part
    own = low

    def at(offset, rows):
        return pl.ds(pl.multiple_of(offset, 16), rows)

    started = []

    def scatter_copy(p, k, d):
        target = lax.rem(digits[k] + d, radices[k])
        return pltpu.make_async_remote_copy(
            src_ref=send.at[p, at(lows[k] + target * parts[k], parts[k])], dst_ref=landing[k].at[p, d - 1],
            send_sem=rsend.at[p, k, d], recv_sem=rrecv.at[p, k, d],
            device_id={"strip": partners[k][d - 1]}, device_id_type=MESH)

    def bias_copy(k, d):
        return pltpu.make_async_remote_copy(
            src_ref=bstage.at[k], dst_ref=blanding[k].at[digits[k]],
            send_sem=bsend.at[k, d], recv_sem=brecv.at[k, d],
            device_id={"strip": partners[k][d - 1]}, device_id_type=MESH)

    def go(copy):
        copy.start()
        started.append(copy)

    def scatter_start(p, k):
        for d in range(1, radices[k]):
            target = lax.rem(digits[k] + d, radices[k])
            rows = at(lows[k] + target * parts[k], parts[k])
            send[p, rows, :] = acc[p, rows, :].astype(BF16)
            go(scatter_copy(p, k, d))
        if p == 0:
            for d in range(1, radices[k]):
                go(bias_copy(k, d))
            blanding[k][digits[k]] = bstage[k]

    def scatter_finish(p, k):
        rows = at(lows[k] + digits[k] * parts[k], parts[k])
        got = acc[p, rows, :]
        for d in range(1, radices[k]):
            scatter_copy(p, k, d).wait_recv()
            got = got + landing[k][p, d - 1].astype(F32)
        acc[p, rows, :] = got
        if p == 0:
            for d in range(1, radices[k]):
                bias_copy(k, d).wait_recv()
            bstage[k + 1] = jnp.sum(blanding[k][...], axis=0)

    def gather_copy(p, k, d, back):
        digit = lax.rem(digits[k] + radices[k] - d, radices[k]) if back else digits[k]
        rows = at(lows[k] + digit * parts[k], parts[k])
        return pltpu.make_async_remote_copy(
            src_ref=total.at[p, rows], dst_ref=total.at[p, rows],
            send_sem=asend.at[p, k, d], recv_sem=arecv.at[p, k, d],
            device_id={"strip": partners[k][d - 1]}, device_id_type=MESH)

    def hop(p, k):
        scatter_finish(p, k)
        if k + 1 < n_st:
            scatter_start(p, k + 1)
        else:
            rows = at(own, chunk)
            total[p, rows, :] = acc[p, rows, :].astype(BF16)
            for d in range(1, radices[k]):
                go(gather_copy(p, k, d, False))

    def back(p, k):
        for d in range(1, radices[k]):
            gather_copy(p, k, d, True).wait_recv()
        if k > 0:
            for d in range(1, radices[k - 1]):
                go(gather_copy(p, k - 1, d, False))

    def chain(p):
        return [functools.partial(hop, p, k) for k in range(n_st)] + [
            functools.partial(back, p, k) for k in reversed(range(n_st))]

    chains = [chain(0), chain(1)]

    def run_next(p):
        if chains[p]:
            chains[p].pop(0)()

    kernel_sums((0, 1))
    spread(0, 3 * ch, 0)
    scatter_start(0, 0)
    kernel_sums((2, 3))
    run_next(0)
    spread(1, 0, 1)
    spread(1, 3 * ch, 2)
    scatter_start(1, 0)
    edge_wait(g_copies)

    for s in range(slots):
        c = jnp.maximum(pos_ref[s], 0)
        act = (pos_ref[s] >= 0).astype(F32)
        inner_l = (c > 0).astype(F32)
        inner_r = (c < slots - 1).astype(F32)
        lc, rc = jnp.maximum(c - 1, 0), jnp.minimum(c + 1, slots - 1)
        put_halo(halo_g, s, c, inner_l, inner_r)

        def build(i, carry):
            m = i * PAIRS
            for f in range(frames):
                for t in range(2):
                    q = pl.ds(m + t, PAIRS)
                    put(s, f, q, 1 - t, gp[c, f, q, 1 - t],
                        last_col(gp[lc, f, q, 1 - t, tail], inner_l),
                        first_col(gp[rc, f, q, 1 - t, head], inner_r))
            return carry

        lax.fori_loop(0, steps, build, 0)

        def second(i, carry):
            m = i * PAIRS
            for f in range(frames):
                res = (jnp.dot(four(s, f, m), wb[...], preferred_element_type=F32) * act).astype(BF16)
                for t in range(2):
                    out_ref[s, f, pl.ds(m, PAIRS), t] = res[:, t * ch:(t + 1) * ch].reshape(PAIRS, width, ch)
            return carry

        lax.fori_loop(0, steps, second, 0)
        run_next(0)
        run_next(1)
    while chains[0] or chains[1]:
        run_next(0)
        run_next(1)

    tot_ref[...] = total[:, :6 * ch, :]
    db_ref[...] = bstage[n_st]
    for copy in started:
        copy.wait_send()


def finish(scale, gi_ref, tot_ref, sum_ref, out_ref, ds_ref, dt_ref, db_ref, ds, dt, db, sems):
    ch = ds.shape[-1]
    tiles = pltpu.make_async_copy(gi_ref, out_ref, sems.at[0])
    tiles.start()
    for k in range(3):
        dt[k] = tot_ref[0, k * ch:(k + 1) * ch, :].astype(F32) * scale
        ds[k] = tot_ref[0, (3 + k) * ch:(4 + k) * ch, :].astype(F32) * scale
    for k in range(6):
        ds[3 + k] = tot_ref[1, k * ch:(k + 1) * ch, :].astype(F32) * scale
    db[...] = jnp.sum(sum_ref[...], axis=0, keepdims=True) * scale
    copies = [
        pltpu.make_async_copy(src, dst, sems.at[1 + i])
        for i, (src, dst) in enumerate(((ds, ds_ref), (dt, dt_ref), (db, db_ref)))
    ]
    for copy in copies:
        copy.start()
    for copy in copies:
        copy.wait()
    tiles.wait()


def per_device(size, x_tiles, grad_out, tile_pos, w_spatial, conv_bias, w_temporal):
    slots, frames, height, width, ch = x_tiles.shape
    half = height // 2
    radices = radices_of(size)
    rows = 6 * ch
    chunk = -(-rows // (size * 16)) * 16
    full = chunk * size
    scale = float(size * slots * frames * height * height) ** -0.5
    cells = frames * half * width
    paired = (slots, frames, half, 2, width, ch)
    edge = (2, slots, frames, width, ch)
    landing, part = [], full
    for radix in radices:
        part //= radix
        landing.append(pltpu.VMEM((2, radix - 1, part, ch), BF16))
    most = max(radices)
    vmem = pl.BlockSpec(memory_space=pltpu.VMEM)
    smem = pl.BlockSpec(memory_space=pltpu.SMEM)
    anywhere = pl.BlockSpec(memory_space=pl.ANY)
    grads, totals, bias_sum = pl.pallas_call(
        functools.partial(kernel, size, radices, chunk),
        out_shape=(
            jax.ShapeDtypeStruct(paired, BF16),
            jax.ShapeDtypeStruct((2, 6 * ch, ch), BF16),
            jax.ShapeDtypeStruct((8, ch), F32),
        ),
        in_specs=[anywhere, anywhere, smem, anywhere, anywhere, anywhere],
        out_specs=(vmem, vmem, vmem),
        scratch_shapes=[
            pltpu.VMEM(paired, BF16),
            pltpu.VMEM(paired, BF16),
            pltpu.VMEM((9, ch, ch), BF16),
            pltpu.VMEM((1, ch), F32),
            pltpu.VMEM((3, ch, ch), BF16),
            pltpu.SemaphoreType.DMA((5,)),
            pltpu.VMEM((12 * ch, 2 * ch), BF16),
            pltpu.VMEM((12 * ch, 2 * ch), BF16),
            pltpu.VMEM((2 * ch, 2 * ch), BF16),
            pltpu.VMEM((slots, frames, half + 1, 2, width, 3 * ch), BF16),
            pltpu.VMEM((slots, frames, half + 1, 2, width, ch), BF16),
            pltpu.VMEM((slots, cells, 2 * ch), BF16),
            pltpu.VMEM((cells, 2 * ch), BF16),
            pltpu.VMEM((cells, 2 * ch), BF16),
            pltpu.VMEM((4, 2 * ch, 3 * ch), F32),
            pltpu.VMEM((2 * ch, 2 * ch), F32),
            pltpu.VMEM((8, 2 * ch), F32),
            pltpu.VMEM(edge, BF16),
            pltpu.VMEM(edge, BF16),
            pltpu.VMEM(edge, BF16),
            pltpu.VMEM(edge, BF16),
            pltpu.VMEM((2, full, ch), F32),
            pltpu.VMEM((2, full, ch), BF16),
            pltpu.VMEM((2, full, ch), BF16),
            pltpu.VMEM((len(radices) + 1, 8, ch), F32),
            *landing,
            *[pltpu.VMEM((radix, 8, ch), F32) for radix in radices],
            pltpu.SemaphoreType.DMA((2,)),
            pltpu.SemaphoreType.DMA((2,)),
            pltpu.SemaphoreType.DMA((2,)),
            pltpu.SemaphoreType.DMA((2,)),
            pltpu.SemaphoreType.DMA((2, len(radices), most)),
            pltpu.SemaphoreType.DMA((2, len(radices), most)),
            pltpu.SemaphoreType.DMA((2, len(radices), most)),
            pltpu.SemaphoreType.DMA((2, len(radices), most)),
            pltpu.SemaphoreType.DMA((len(radices), most)),
            pltpu.SemaphoreType.DMA((len(radices), most)),
        ],
        compiler_params=pltpu.CompilerParams(
            collective_id=0, has_side_effects=True, vmem_limit_bytes=48 * 2**20
        ),
    )(
        x_tiles.reshape(paired),
        grad_out.reshape(paired),
        tile_pos,
        w_spatial,
        conv_bias.reshape(1, ch),
        w_temporal,
    )
    grad_in, d_spatial, d_temporal, d_bias = pl.pallas_call(
        functools.partial(finish, scale),
        out_shape=(
            jax.ShapeDtypeStruct(paired, BF16),
            jax.ShapeDtypeStruct((9, ch, ch), F32),
            jax.ShapeDtypeStruct((3, ch, ch), F32),
            jax.ShapeDtypeStruct((1, ch), F32),
        ),
        in_specs=[anywhere, vmem, vmem],
        out_specs=(anywhere, anywhere, anywhere, anywhere),
        scratch_shapes=[
            pltpu.VMEM((9, ch, ch), F32),
            pltpu.VMEM((3, ch, ch), F32),
            pltpu.VMEM((1, ch), F32),
            pltpu.SemaphoreType.DMA((4,)),
        ],
    )(grads, totals, bias_sum)
    return grad_in.reshape(x_tiles.shape), d_spatial, d_temporal, d_bias.reshape(ch)


def solution(mesh):
    tiles = P(("groups", "strip"), None, None, None, None)
    in_specs = (tiles, tiles, P(("groups", "strip")), P(), P(), P())
    out_specs = (tiles, P("groups", None, None), P("groups", None, None), P("groups"))
    return jax.shard_map(
        functools.partial(per_device, mesh.shape["strip"]),
        mesh=mesh, in_specs=in_specs, out_specs=out_specs, check_vma=False,
    )
```

time: 56 us -> 119 us (2.12)
  Pallas kernels: 47 us -> 111 us
    pallas_call x1 -> x2, Pallas kernels: 47 us -> 111 us  [the longest x1 65.7 us: per_device(): pl.pallas_call(functools.partial(finish, scale), out_shape=(jax.ShapeDtyp...]
    unnamed x14 -> x16, local copies, waits for them, and re-layouts: 8.07 us -> 7.42 us
where the time goes in v2:
time: 119 us
  Pallas kernels  111 us (93%)
  local copies, waits for them, and re-layouts  7.42 us (6%)
    pallas_call x1, Pallas kernels, per_device(): pl.pallas_call(functools.partial(finish, scale), out_shape=(jax.ShapeDtyp...  65.7 us
    pallas_call x1, Pallas kernels, per_device(): pl.pallas_call(functools.partial(kernel, size, radices, chunk), out_shape...  45.1 us
    unnamed x16, local copies, waits for them, and re-layouts  7.42 us

profile of v2, /device:TPU:0, one launch (start us, length us, event | category | flops | bytes accessed | tf_op | source)
XLA Modules:
  0.0 118.9 jit_solution(14992935853362475992)
XLA Ops:
  0.6 0.0 copy-start
  0.6 1.6 %copy-done = bf16[4,2,32,32,128]{4,3,2,1,0:T(8,128)(2,1)S(1)} copy-done((bf16[4,2,32,32,128]{4,3,2,1,0:T(8,128)(2,1)S(1)}, bf16[4,2,32,32,128]{4,3,2,1,0:T(8,128)(2,1)}, u32[]{:S(2)}) %copy-start) | copy-done | bytes 2097176
  2.2 0.0 copy-start.3
  2.2 1.0 copy-done.3
  3.2 0.0 copy-start.4
  3.2 0.9 copy-done.4
  4.1 0.0 copy-start.6
  4.1 0.7 copy-done.6
  4.7 0.0 copy-start.7
  4.7 0.7 copy-done.7
  5.4 45.1 %shard_map.93 = (bf16[4,2,16,2,32,128]{5,4,3,2,1,0:T(8,128)(2,1)S(1)}, bf16[2,768,128]{2,1,0:T(8,128)(2,1)S(1)}, f32[8,128]{1,0:T(8,128)S(1)}) custom-call(bf16[4,2,16,2,32,128]{5,4,3,2,1,0:T(8,128)(2,1)S(1)} %bitcast.5, bf16[4,2,16,2,32,128]{5,4,3,2,1,0:T(8,128)(2,1)} %bitcast.7, s32[4]{0:T(128)S(1)} %copy-done.6, bf16[9,128,128]{2,1,0:T(8,128)(2,1)S(1)} %copy-done.3, ...), custom_call_target="tpu_custom_call" | custom-call | tf_op jit(solution)/shard_map/pallas_call | solution.py:452
  50.5 0.0 copy-start.1
  50.5 1.3 %copy-done.1 = bf16[4,2,16,2,32,128]{5,4,3,2,1,0:T(8,128)(2,1)} copy-done((bf16[4,2,16,2,32,128]{5,4,3,2,1,0:T(8,128)(2,1)}, bf16[4,2,16,2,32,128]{5,4,3,2,1,0:T(8,128)(2,1)S(1)}, u32[]{:S(2)}) %copy-start.1) | copy-done | bytes 2097176
  51.9 0.0 copy-start.2
  51.9 0.7 copy-done.2
  52.6 0.0 copy-start.5
  52.6 0.6 copy-done.5
  53.2 65.7 %shard_map.94 = (bf16[4,2,16,2,32,128]{5,4,3,2,1,0:T(8,128)(2,1)}, f32[9,128,128]{2,1,0:T(8,128)}, f32[3,128,128]{2,1,0:T(8,128)}, f32[1,128]{1,0:T(1,128)}) custom-call(bf16[4,2,16,2,32,128]{5,4,3,2,1,0:T(8,128)(2,1)} %copy-done.1, bf16[2,768,128]{2,1,0:T(8,128)(2,1)} %copy-done.2, f32[8,128]{1,0:T(8,128)} %copy-done.5), custom_call_target="tpu_custom_call" | custom-call | tf_op jit(solution)/shard_map/pallas_call | solution.py:511
Async XLA Ops:
  0.6 1.6 %copy-start = (bf16[4,2,32,32,128]{4,3,2,1,0:T(8,128)(2,1)S(1)}, bf16[4,2,32,32,128]{4,3,2,1,0:T(8,128)(2,1)}, u32[]{:S(2)}) copy-start(bf16[4,2,32,32,128]{4,3,2,1,0:T(8,128)(2,1)} %param.6) | copy-start | bytes 6291460
  2.2 1.0 copy-start.3
  3.2 0.9 copy-start.4
  4.1 0.7 copy-start.6
  4.7 0.7 copy-start.7
  50.5 1.3 %copy-start.1 = (bf16[4,2,16,2,32,128]{5,4,3,2,1,0:T(8,128)(2,1)}, bf16[4,2,16,2,32,128]{5,4,3,2,1,0:T(8,128)(2,1)S(1)}, u32[]{:S(2)}) copy-start(bf16[4,2,16,2,32,128]{5,4,3,2,1,0:T(8,128)(2,1)S(1)} %get-tuple-element.11.gi_ref) | copy-start | bytes 6291460
  51.9 0.8 copy-start.2
  52.6 0.6 copy-start.5

commit v3 on v2

--- a/solution.py
+++ b/solution.py
@@ -9,15 +9,11 @@
 
 MESH = pl.DeviceIdType.MESH
 F32, BF16 = jnp.float32, jnp.bfloat16
-PAIRS = 8
+PAIRS = 16
 
 
 def radices_of(size):
     found, rest = [], size
-    for radix in (2, 2):
-        if rest % radix == 0:
-            found.append(radix)
-            rest //= radix
     while rest % 4 == 0:
         found.append(4)
         rest //= 4
@@ -31,7 +27,7 @@
 
 
 def kernel(size, radices, chunk, x_hbm, g_hbm, pos_ref, ws_hbm, bias_hbm, wt_hbm,
-           out_ref, tot_ref, db_ref,
+           out_ref, ds_ref, dt_ref, db_ref,
            x_ref, g_ref, ws_ref, bias_ref, wt_ref, in_sem, wf, wb, wtt, x3, gp, gpa, ha, ga, psum, tsum, bsum, edge_x, edge_g, halo_x, halo_g,
            acc, send, total, bstage, *rest):
     n_st = len(radices)
@@ -362,10 +358,10 @@
     spread(0, 3 * ch, 0)
     scatter_start(0, 0)
     kernel_sums((2, 3))
-    run_next(0)
     spread(1, 0, 1)
     spread(1, 3 * ch, 2)
     scatter_start(1, 0)
+    run_next(0)
     edge_wait(g_copies)
 
     for s in range(slots):
@@ -403,31 +399,14 @@
         run_next(0)
         run_next(1)
 
-    tot_ref[...] = total[:, :6 * ch, :]
+    for k in range(3):
+        dt_ref[k] = total[0, k * ch:(k + 1) * ch, :]
+        ds_ref[k] = total[0, (3 + k) * ch:(4 + k) * ch, :]
+    for k in range(6):
+        ds_ref[3 + k] = total[1, k * ch:(k + 1) * ch, :]
     db_ref[...] = bstage[n_st]
     for copy in started:
         copy.wait_send()
-
-
-def finish(scale, gi_ref, tot_ref, sum_ref, out_ref, ds_ref, dt_ref, db_ref, ds, dt, db, sems):
-    ch = ds.shape[-1]
-    tiles = pltpu.make_async_copy(gi_ref, out_ref, sems.at[0])
-    tiles.start()
-    for k in range(3):
-        dt[k] = tot_ref[0, k * ch:(k + 1) * ch, :].astype(F32) * scale
-        ds[k] = tot_ref[0, (3 + k) * ch:(4 + k) * ch, :].astype(F32) * scale
-    for k in range(6):
-        ds[3 + k] = tot_ref[1, k * ch:(k + 1) * ch, :].astype(F32) * scale
-    db[...] = jnp.sum(sum_ref[...], axis=0, keepdims=True) * scale
-    copies = [
-        pltpu.make_async_copy(src, dst, sems.at[1 + i])
-        for i, (src, dst) in enumerate(((ds, ds_ref), (dt, dt_ref), (db, db_ref)))
-    ]
-    for copy in copies:
-        copy.start()
-    for copy in copies:
-        copy.wait()
-    tiles.wait()
 
 
 def per_device(size, x_tiles, grad_out, tile_pos, w_spatial, conv_bias, w_temporal):
@@ -448,16 +427,17 @@
     most = max(radices)
     vmem = pl.BlockSpec(memory_space=pltpu.VMEM)
     smem = pl.BlockSpec(memory_space=pltpu.SMEM)
-    anywhere = pl.BlockSpec(memory_space=pl.ANY)
-    grads, totals, bias_sum = pl.pallas_call(
+    hbm = pl.BlockSpec(memory_space=pltpu.HBM)
+    grads, d_spatial, d_temporal, bias_sum = pl.pallas_call(
         functools.partial(kernel, size, radices, chunk),
         out_shape=(
             jax.ShapeDtypeStruct(paired, BF16),
-            jax.ShapeDtypeStruct((2, 6 * ch, ch), BF16),
+            jax.ShapeDtypeStruct((9, ch, ch), BF16),
+            jax.ShapeDtypeStruct((3, ch, ch), BF16),
             jax.ShapeDtypeStruct((8, ch), F32),
         ),
-        in_specs=[anywhere, anywhere, smem, anywhere, anywhere, anywhere],
-        out_specs=(vmem, vmem, vmem),
+        in_specs=[hbm, hbm, smem, hbm, hbm, hbm],
+        out_specs=(vmem, vmem, vmem, vmem),
         scratch_shapes=[
             pltpu.VMEM(paired, BF16),
             pltpu.VMEM(paired, BF16),
@@ -508,24 +488,10 @@
         conv_bias.reshape(1, ch),
         w_temporal,
     )
-    grad_in, d_spatial, d_temporal, d_bias = pl.pallas_call(
-        functools.partial(finish, scale),
-        out_shape=(
-            jax.ShapeDtypeStruct(paired, BF16),
-            jax.ShapeDtypeStruct((9, ch, ch), F32),
-            jax.ShapeDtypeStruct((3, ch, ch), F32),
-            jax.ShapeDtypeStruct((1, ch), F32),
-        ),
-        in_specs=[anywhere, vmem, vmem],
-        out_specs=(anywhere, anywhere, anywhere, anywhere),
-        scratch_shapes=[
-            pltpu.VMEM((9, ch, ch), F32),
-            pltpu.VMEM((3, ch, ch), F32),
-            pltpu.VMEM((1, ch), F32),
-            pltpu.SemaphoreType.DMA((4,)),
-        ],
-    )(grads, totals, bias_sum)
-    return grad_in.reshape(x_tiles.shape), d_spatial, d_temporal, d_bias.reshape(ch)
+    d_spatial = d_spatial.astype(F32) * scale
+    d_temporal = d_temporal.astype(F32) * scale
+    d_bias = jnp.sum(bias_sum, axis=0) * scale
+    return grads.reshape(x_tiles.shape), d_spatial, d_temporal, d_bias
 
 
 def solution(mesh):

time: 119 us -> 48.9 us (0.41)
  Pallas kernels: 111 us -> 39.8 us
  other arithmetic: 0 us -> 2.1 us
  local copies, waits for them, and re-layouts: 7.42 us -> 6.07 us
    pallas_call x1 -> x0, Pallas kernels: 65.7 us -> none  [per_device(): pl.pallas_call(functools.partial(finish, scale), out_shape=(jax.ShapeDtyp...]
    pallas_call x1, Pallas kernels: 45.1 us -> 39.8 us  [per_device(): pl.pallas_call(functools.partial(kernel, size, radices, chunk), out_shape...]
    mul x0 -> x3, other arithmetic: none -> 2.08 us  [the longest x1 0.87 us: per_device(): d_spatial = d_spatial.astype(F32) * scale]
    unnamed x16 -> x11, local copies, waits for them, and re-layouts: 7.42 us -> 6.07 us
where the time goes in v3:
time: 48.9 us; the launch traced here: 48.6 us
  Pallas kernels  39.8 us (81%)
  local copies, waits for them, and re-layouts  6.07 us (12%)
  other arithmetic  2.1 us (4%)
  between operations  0.66 us (1%)
    pallas_call x1, Pallas kernels, per_device(): pl.pallas_call(functools.partial(kernel, size, radices, chunk), out_shape...  39.8 us
    unnamed x11, local copies, waits for them, and re-layouts  6.07 us

profile of v3, /device:TPU:0, one launch (start us, length us, event | category | flops | bytes accessed | tf_op | source)
XLA Modules:
  0.0 48.6 jit_solution(1059602938762661341)
XLA Ops:
  0.6 0.0 copy-start
  0.6 1.6 %copy-done = bf16[4,2,32,32,128]{4,3,2,1,0:T(8,128)(2,1)S(1)} copy-done((bf16[4,2,32,32,128]{4,3,2,1,0:T(8,128)(2,1)S(1)}, bf16[4,2,32,32,128]{4,3,2,1,0:T(8,128)(2,1)}, u32[]{:S(2)}) %copy-start) | copy-done | bytes 2097176
  2.2 0.0 copy-start.1
  2.2 1.0 %copy-done.1 = bf16[9,128,128]{2,1,0:T(8,128)(2,1)S(1)} copy-done((bf16[9,128,128]{2,1,0:T(8,128)(2,1)S(1)}, bf16[9,128,128]{2,1,0:T(8,128)(2,1)}, u32[]{:S(2)}) %copy-start.1) | copy-done | bytes 294936
  3.2 0.0 copy-start.2
  3.2 0.9 %copy-done.2 = bf16[3,128,128]{2,1,0:T(8,128)(2,1)S(1)} copy-done((bf16[3,128,128]{2,1,0:T(8,128)(2,1)S(1)}, bf16[3,128,128]{2,1,0:T(8,128)(2,1)}, u32[]{:S(2)}) %copy-start.2) | copy-done | bytes 98328
  4.1 0.0 copy-start.3
  4.1 0.7 %copy-done.3 = s32[4]{0:T(128)S(1)} copy-done((s32[4]{0:T(128)S(1)}, s32[4]{0:T(128)}, u32[]{:S(2)}) %copy-start.3) | copy-done | bytes 40
  4.7 0.0 copy-start.4
  4.7 0.7 %copy-done.4 = f32[128]{0:T(128)S(1)} copy-done((f32[128]{0:T(128)S(1)}, f32[128]{0:T(128)}, u32[]{:S(2)}) %copy-start.4) | copy-done | bytes 536
  5.4 39.8 %shard_map.93 = (bf16[4,2,16,2,32,128]{5,4,3,2,1,0:T(8,128)(2,1)S(1)}, bf16[9,128,128]{2,1,0:T(8,128)(2,1)S(1)}, bf16[3,128,128]{2,1,0:T(8,128)(2,1)S(1)}, f32[8,128]{1,0:T(8,128)S(1)}) custom-call(bf16[4,2,16,2,32,128]{5,4,3,2,1,0:T(8,128)(2,1)S(1)} %bitcast.4, bf16[4,2,16,2,32,128]{5,4,3,2,1,0:T(8,128)(2,1)} %bitcast.7, s32[4]{0:T(128)S(1)} %copy-done.3, ...), custom_call_target="tpu_custom_call" | custom-call | tf_op jit(solution)/shard_map/pallas_call | solution.py:431
  45.2 0.5 %broadcast_multiply_fusion = f32[128]{0:T(128)} fusion(f32[128]{0:T(128)S(1)} %reduce_sum.9), kind=kLoop, calls=%fused_computation.2 | loop fusion | flops 128 | bytes 1024 | tf_op jit(solution)/shard_map/mul | solution.py:493
  45.8 0.7 %convert_multiply_fusion.1 = f32[3,128,128]{2,1,0:T(8,128)} fusion(bf16[3,128,128]{2,1,0:T(8,128)(2,1)S(1)} %get-tuple-element.10), kind=kLoop, calls=%fused_computation.1 | loop fusion | flops 98304 | bytes 294912 | tf_op jit(solution)/shard_map/mul | solution.py:492
  46.4 0.9 %convert_multiply_fusion = f32[9,128,128]{2,1,0:T(8,128)} fusion(bf16[9,128,128]{2,1,0:T(8,128)(2,1)S(1)} %get-tuple-element.9), kind=kLoop, calls=%fused_computation | loop fusion | flops 294912 | bytes 884736 | tf_op jit(solution)/shard_map/mul | solution.py:491
  47.3 1.3 %copy.11 = bf16[4,2,32,32,128]{4,3,2,1,0:T(8,128)(2,1)} copy(bf16[4,2,32,32,128]{4,3,2,1,0:T(8,128)(2,1)S(1)} %bitcast.5) | data formatting | bytes 4194304
  (1 shorter events, 0.0 us)
Async XLA Ops:
  0.6 1.6 %copy-start = (bf16[4,2,32,32,128]{4,3,2,1,0:T(8,128)(2,1)S(1)}, bf16[4,2,32,32,128]{4,3,2,1,0:T(8,128)(2,1)}, u32[]{:S(2)}) copy-start(bf16[4,2,32,32,128]{4,3,2,1,0:T(8,128)(2,1)} %param.6) | copy-start | bytes 6291460
  2.2 1.0 %copy-start.1 = (bf16[9,128,128]{2,1,0:T(8,128)(2,1)S(1)}, bf16[9,128,128]{2,1,0:T(8,128)(2,1)}, u32[]{:S(2)}) copy-start(bf16[9,128,128]{2,1,0:T(8,128)(2,1)} %ws_hbm.1) | copy-start | bytes 884740
  3.2 0.9 %copy-start.2 = (bf16[3,128,128]{2,1,0:T(8,128)(2,1)S(1)}, bf16[3,128,128]{2,1,0:T(8,128)(2,1)}, u32[]{:S(2)}) copy-start(bf16[3,128,128]{2,1,0:T(8,128)(2,1)} %wt_hbm.1) | copy-start | bytes 294916
  4.1 0.7 %copy-start.3 = (s32[4]{0:T(128)S(1)}, s32[4]{0:T(128)}, u32[]{:S(2)}) copy-start(s32[4]{0:T(128)} %pos_ref.1) | copy-start | bytes 52
  4.7 0.7 %copy-start.4 = (f32[128]{0:T(128)S(1)}, f32[128]{0:T(128)}, u32[]{:S(2)}) copy-start(f32[128]{0:T(128)} %param.10) | copy-start | bytes 1540
